TPU v7x, 32 devices: a whole 2x2x4 slice. The times are simulated.
32 devices in a mesh: dp: 8 (over z, x), mp: 4 (over y, core).
Axes of the slice: x: 2, y: 2, z: 4, core: 2. Of those that a mesh axis runs over, the one named last changes fastest.
Arguments:
- layer_input: bfloat16 [4096, 4096], P('dp'), may hold values from -40 to 40
- gate_pre: bfloat16 [4096, 5120], P('dp', 'mp'), may hold values from -5 to 5
- up_pre: bfloat16 [4096, 5120], P('dp', 'mp'), may hold values from -5 to 5
- hidden_cot: bfloat16 [4096, 5120], P('dp', 'mp'), may hold values from -6 to 6
- teacher_ids: int32 [4096], P('dp'), may hold values from 0 to 63
- adv_table: float32 [64], replicated, may hold values from 0.25 to 2
- gate_weight: bfloat16 [4096, 5120], P('dp', 'mp'), may hold values from -0.09375 to 0.09375
- up_weight: bfloat16 [4096, 5120], P('dp', 'mp'), may hold values from -0.09375 to 0.09375
- row_moments: float32 [2, 4096], P(None, 'dp'), may hold values from 0.05 to 0.5
- col_moments: float32 [2, 5120], P(None, 'mp'), may hold values from 0.05 to 0.5
Outputs:
- input_grad: bfloat16 [4096, 4096], P('dp', 'mp')
- gate_update: float32 [4096, 5120], P('dp', 'mp')
- up_update: float32 [4096, 5120], P('dp', 'mp')
- new_rows: float32 [2, 4096], P(None, 'dp')
- new_cols: float32 [2, 5120], P(None, 'mp')
All inputs are finite; a program needn't handle non-finite values.
Results may differ from a plain program's by a relative error of at most 0.011.
Values may be sent and summed in bfloat16 or wider, within the bound.
No kernel may reach another device: no remote copies, remote signals or barrier semaphores. Data moves between devices by JAX's collectives and lax.ppermute only.
A program may use at most 192 MiB of HBM per device.

v0:
```python
import math

import jax
import jax.numpy as jnp
from jax import lax
from jax.sharding import PartitionSpec as P

decay_rate = 0.9
tanh_scale = math.sqrt(2.0 / math.pi)
cubic_term = 0.044715


def gelu_pair(pre_act):
    argument = tanh_scale * (pre_act + cubic_term * pre_act * pre_act * pre_act)
    tangent = jnp.tanh(argument)
    gelu_value = 0.5 * pre_act * (1.0 + tangent)
    gelu_slope = 0.5 * (1.0 + tangent) + 0.5 * pre_act * (1.0 - tangent * tangent) * tanh_scale * (
        1.0 + 3.0 * cubic_term * pre_act * pre_act
    )
    return (gelu_value, gelu_slope)


def local(
    layer_input,
    gate_pre,
    up_pre,
    hidden_cot,
    teacher_ids,
    adv_table,
    gate_weight,
    up_weight,
    row_moments,
    col_moments,
):
    data_size = lax.axis_size("dp")
    model_size = lax.axis_size("mp")
    block_rows = gate_weight.shape[0]
    block_cols = gate_weight.shape[1]
    token_count = layer_input.shape[0]
    classes = adv_table.shape[0]
    class_hit = teacher_ids[:, None] == jnp.arange(classes, dtype=jnp.int32)[None, :]
    advantage = jnp.sum(jnp.where(class_hit, adv_table[None, :], 0.0), axis=1)
    weighted = hidden_cot.astype(jnp.float32) * advantage[:, None]
    gelu_value, gelu_slope = gelu_pair(gate_pre.astype(jnp.float32))
    gate_grad = (weighted * up_pre.astype(jnp.float32) * gelu_slope).astype(jnp.bfloat16)
    up_grad = (weighted * gelu_value).astype(jnp.bfloat16)
    contract_last = (((1,), (1,)), ((), ()))
    contract_first = (((0,), (0,)), ((), ()))
    pieces = lax.all_gather((gate_weight, up_weight), "dp", axis=0, tiled=True)
    partial_sum = lax.dot_general(
        gate_grad, pieces[0], contract_last, preferred_element_type=jnp.float32
    ) + lax.dot_general(up_grad, pieces[1], contract_last, preferred_element_type=jnp.float32)
    input_grad = lax.psum_scatter(
        partial_sum.astype(jnp.bfloat16), "mp", scatter_dimension=1, tiled=True
    )
    grad_scale = 1.0 / math.sqrt(token_count * data_size)
    gate_term = lax.dot_general(
        layer_input, gate_grad, contract_first, preferred_element_type=jnp.float32
    )
    up_term = lax.dot_general(
        layer_input, up_grad, contract_first, preferred_element_type=jnp.float32
    )
    summed = lax.psum_scatter(
        jnp.concatenate([gate_term, up_term], axis=1).astype(jnp.bfloat16),
        "dp",
        scatter_dimension=0,
        tiled=True,
    ).astype(jnp.float32)
    grad_gate = summed[:, :block_cols] * grad_scale
    grad_up = summed[:, block_cols:] * grad_scale
    squares_gate = grad_gate * grad_gate
    squares_up = grad_up * grad_up
    row_local = jnp.stack([jnp.sum(squares_gate, axis=1), jnp.sum(squares_up, axis=1)])
    col_local = jnp.stack([jnp.sum(squares_gate, axis=0), jnp.sum(squares_up, axis=0)])
    row_total = lax.psum(row_local, "mp")
    col_total = lax.psum(col_local, "dp")
    new_rows = decay_rate * row_moments + (1.0 - decay_rate) * (
        row_total / (block_cols * model_size)
    )
    new_cols = decay_rate * col_moments + (1.0 - decay_rate) * (
        col_total / (block_rows * data_size)
    )
    scaled_gate = grad_gate / jnp.sqrt(new_rows[0][:, None] * new_cols[0][None, :])
    scaled_up = grad_up / jnp.sqrt(new_rows[1][:, None] * new_cols[1][None, :])
    square_sums = lax.psum(
        jnp.stack([jnp.sum(scaled_gate * scaled_gate), jnp.sum(scaled_up * scaled_up)]),
        ("dp", "mp"),
    )
    entry_count = block_rows * data_size * block_cols * model_size
    mean_square = square_sums / entry_count
    gate_update = scaled_gate / jnp.sqrt(mean_square[0] + 1e-06)
    up_update = scaled_up / jnp.sqrt(mean_square[1] + 1e-06)
    return (input_grad, gate_update, up_update, new_rows, new_cols)


def solution(mesh):
    in_specs = (
        P("dp", None),
        P("dp", "mp"),
        P("dp", "mp"),
        P("dp", "mp"),
        P("dp"),
        P(),
        P("dp", "mp"),
        P("dp", "mp"),
        P(None, "dp"),
        P(None, "mp"),
    )
    out_specs = (P("dp", "mp"), P("dp", "mp"), P("dp", "mp"), P(None, "dp"), P(None, "mp"))
    return jax.shard_map(local, mesh=mesh, in_specs=in_specs, out_specs=out_specs, check_vma=False)
```

profile of v0, /device:TPU:1, one launch (start us, length us, event | category | flops | bytes accessed | tf_op | source)
XLA Modules:
  0.0 766.3 jit_solution(3874818478631827464)
XLA Ops:
  7.2 0.0 all-gather.3.cloned.1.call-start
  7.2 0.7 all-gather.3.cloned.1.call-update
  7.9 0.0 all-gather.5.cloned.1.call-start
  8.0 0.7 all-gather.5.cloned.1.call-update
  8.7 0.0 reduce-scatter.5.cloned.1.call-start
  8.7 0.1 select_reduce_fusion
  8.9 0.0 copy-start.7
  8.9 9.0 %fusion.1 = bf16[4096,1280]{0,1:T(8,128)(2,1)S(1)} fusion(bf16[512,4096]{1,0:T(8,128)(2,1)} %param.10, bf16[512,1280]{1,0:T(8,128)(2,1)S(1)} %copy-done.8, bf16[512,1280]{1,0:T(8,128)(2,1)} %param.13, f32[512]{0:T(512)S(1)} %select_reduce_fusion), kind=kOutput, calls=%fused_computation.4 | convolution fusion | flops 5382471680 | bytes 17303552 | tf_op jit(solution)/shard_map/dot_general | solution.py:60
  17.9 10.0 %fusion = bf16[4096,1280]{0,1:T(8,128)(2,1)S(1)} fusion(bf16[512,4096]{1,0:T(8,128)(2,1)} %param.10, bf16[512,1280]{1,0:T(8,128)(2,1)S(1)} %copy-done.8, bf16[512,1280]{1,0:T(8,128)(2,1)S(1)} %copy-done.7, bf16[512,1280]{1,0:T(8,128)(2,1)} %param.13, f32[512]{0:T(512)S(1)} %select_reduce_fusion), kind=kOutput, calls=%fused_computation.3 | convolution fusion | flops 5389680640 | bytes 18614272 | tf_op jit(solution)/shard_map/dot_general | solution.py:57
  27.9 17.6 %pad_maximum_fusion = bf16[4096,2560]{0,1:T(8,128)(2,1)} fusion(bf16[4096,1280]{0,1:T(8,128)(2,1)S(1)} %fusion.1, bf16[4096,1280]{0,1:T(8,128)(2,1)S(1)} %fusion), kind=kLoop, calls=%fused_computation | loop fusion | flops 41943040 | bytes 41943040 | tf_op jit(solution)/shard_map/concatenate | solution.py:64
  45.5 0.0 reduce-scatter.5.cloned.1.call-update
  45.6 0.2 reduce-scatter.3.cloned.1.call-start
  45.8 117.0 %all-gather.3.cloned.1.call-done = bf16[4096,1280]{1,0:T(8,128)(2,1)} async-done(((bf16[512,1280]{1,0:T(8,128)(2,1)}), bf16[4096,1280]{1,0:T(8,128)(2,1)}) %all-gather.3.cloned.1.call-update) | async-done | bytes 10485776 | tf_op jit(solution)/shard_map/all_gather | solution.py:49
  162.8 14.0 %fusion.19 = f32[512,4096]{1,0:T(8,128)} fusion(bf16[4096,1280]{1,0:T(8,128)(2,1)} %all-gather.3.cloned.1.call-done, bf16[512,1280]{1,0:T(8,128)(2,1)S(1)} %copy-done.8, bf16[512,1280]{1,0:T(8,128)(2,1)S(1)} %copy-done.7, bf16[512,1280]{1,0:T(8,128)(2,1)} %param.13, f32[512]{0:T(512)S(1)} %select_reduce_fusion), kind=kOutput, calls=%fused_computation.48 | convolution fusion | flops 5384437760 | bytes 22808576 | tf_op jit(solution)/shard_map/dot_general | solution.py:50
  176.7 137.3 %all-gather.5.cloned.1.call-done = bf16[4096,1280]{1,0:T(8,128)(2,1)} async-done(((bf16[512,1280]{1,0:T(8,128)(2,1)}), bf16[4096,1280]{1,0:T(8,128)(2,1)}) %all-gather.5.cloned.1.call-update) | async-done | bytes 10485776 | tf_op jit(solution)/shard_map/all_gather | solution.py:49
  314.0 13.3 %add_convert_fusion = bf16[512,4096]{1,0:T(8,128)(2,1)} fusion(f32[512,4096]{1,0:T(8,128)} %fusion.19, bf16[4096,1280]{1,0:T(8,128)(2,1)} %all-gather.5.cloned.1.call-done, bf16[512,1280]{1,0:T(8,128)(2,1)S(1)} %copy-done.8, bf16[512,1280]{1,0:T(8,128)(2,1)} %param.13, f32[512]{0:T(512)S(1)} %select_reduce_fusion), kind=kOutput, calls=%fused_computation.5 | convolution fusion | flops 5381423104 | bytes 25692160 | tf_op jit(solution)/shard_map/dot_general | solution.py:52
  327.3 0.0 reduce-scatter.3.cloned.1.call-update
  327.3 332.9 %reduce-scatter.5.cloned.1.call-done = bf16[512,2560]{0,1:T(8,128)(2,1)} async-done(((bf16[4096,2560]{0,1:T(8,128)(2,1)}), bf16[512,2560]{0,1:T(8,128)(2,1)}) %reduce-scatter.5.cloned.1.call-update) | async-done | bytes 2621456 | tf_op jit(solution)/shard_map/reduce_scatter | solution.py:63
  660.2 2.5 convert_element_type.28
  662.7 0.8 multiply_reduce_fusion.5
  663.4 1.5 copy-done
  665.0 5.6 psum.21
  670.7 28.0 %psum.22 = f32[2,1280]{1,0:T(2,128)S(1)} all-reduce(f32[2,1280]{1,0:T(2,128)S(1)} %pad_maximum_fusion.1), channel_id=1, replica_groups=mesh['dp'=8,'mp'=4] {'dp'}, use_global_device_ids=true, to_apply=%region_8.9 | all-reduce | flops 2560 | bytes 20480 | tf_op jit(solution)/shard_map/psum | solution.py:76
  698.6 0.0 copy-start.1
  698.7 0.0 copy-start.2
  698.7 3.9 multiply_reduce_fusion.1
  702.6 1.4 pad_maximum_fusion.3
  704.0 44.4 %psum.23 = f32[2]{0:T(128)S(1)} all-reduce(f32[2]{0:T(128)S(1)} %pad_maximum_fusion.3), channel_id=1, replica_groups=mesh['dp'=8,'mp'=4] {'dp','mp'}, use_global_device_ids=true, to_apply=%region_11.12 | all-reduce | flops 2 | bytes 16 | tf_op jit(solution)/shard_map/psum | solution.py:85
  748.4 0.6 fusion.22
  750.4 4.1 fusion.15
  754.4 3.2 copy.17
  757.6 2.1 copy.18
  (24 shorter events, 0.1 us)
Async XLA Ops:
  7.2 1.6 copy-start.5
  7.2 1.6 copy-start.6
  7.2 1.7 copy-start.8
  7.2 155.6 %all-gather.3.cloned.1.call-start = ((), (), s32[]{:S(2)}) async-start(), calls=%async_computation.2 | async-start | bytes 11796480 | tf_op jit(solution)/shard_map/all_gather | solution.py:49
  7.9 306.1 %all-gather.5.cloned.1.call-start = ((), (), s32[]{:S(2)}) async-start(), calls=%async_computation.3 | async-start | bytes 11796480 | tf_op jit(solution)/shard_map/all_gather | solution.py:49
  8.7 651.5 %reduce-scatter.5.cloned.1.call-start = ((), (), s32[]{:S(2)}) async-start(), calls=%async_computation.5 | async-start | bytes 23592960 | tf_op jit(solution)/shard_map/reduce_scatter | solution.py:63
  8.9 9.0 %copy-start.7 = (bf16[512,1280]{1,0:T(8,128)(2,1)S(1)}, bf16[512,1280]{1,0:T(8,128)(2,1)}, u32[]{:S(2)}) copy-start(bf16[512,1280]{1,0:T(8,128)(2,1)} %param.12) | copy-start | bytes 3932164
  45.6 714.2 %reduce-scatter.3.cloned.1.call-start = ((), (), s32[]{:S(2)}) async-start(), calls=%async_computation.4 | async-start | bytes 5242880 | tf_op jit(solution)/shard_map/reduce_scatter | solution.py:53
  662.6 2.3 copy-start
  662.7 36.0 %copy-start.3 = (f32[2,1280]{1,0:T(2,128)S(1)}, f32[2,1280]{1,0:T(2,128)}, u32[]{:S(2)}) copy-start(f32[2,1280]{1,0:T(2,128)} %param.19) | copy-start | bytes 30724
  662.7 36.0 %copy-start.4 = (f32[2,512]{1,0:T(2,128)S(1)}, f32[2,512]{1,0:T(2,128)}, u32[]{:S(2)}) copy-start(f32[2,512]{1,0:T(2,128)} %param.18) | copy-start | bytes 12292
  698.6 4.0 copy-start.1
  698.7 3.9 copy-start.2
Sparse Core Ops, SparseCore 0:
  10.2 152.5 all-gather.2
  164.9 149.0 all-gather.4
  317.9 342.2 reduce-scatter.4
  663.1 43.5 reduce-scatter.2
where the time goes:
time: 769 us; the launch traced here: 766 us
  waiting for transfers between devices  589 us (77%)
  blocking collectives  78 us (10%)
  matrix products  46.3 us (6%)
  other arithmetic  30.3 us (4%)
  between operations  15.3 us (2%)
    reduce_scatter x1, waiting for transfers between devices, local(): lax.psum_scatter(jnp.concatenate([gate_term, up_term], axis=1).astype(jnp...  333 us
    all_gather x2, waiting for transfers between devices, local(): pieces = lax.all_gather((gate_weight, up_weight), 'dp', axis=0, tiled=True)  254 us
    psum x1, blocking collectives, local(): lax.psum(jnp.stack([jnp.sum(scaled_gate * scaled_gate), jnp.sum(scaled_up...  44.4 us
    psum x1, blocking collectives, local(): col_total = lax.psum(col_local, 'dp')  28 us
    concatenate x1, other arithmetic, local(): jnp.concatenate([gate_term, up_term], axis=1).astype(jnp.bfloat16)  17.6 us
  transfers between devices with their start and end apart: 4, of which 3 were waited for; matrix products, arithmetic and copies ran while one was open for 11% of the time, Pallas kernels for 0%

commit v1 on v0

--- a/solution.py
+++ b/solution.py
@@ -1,13 +1,20 @@
+import functools
 import math
 
 import jax
 import jax.numpy as jnp
 from jax import lax
+from jax.experimental import pallas as pl
+from jax.experimental.pallas import tpu as pltpu
 from jax.sharding import PartitionSpec as P
 
 decay_rate = 0.9
 tanh_scale = math.sqrt(2.0 / math.pi)
 cubic_term = 0.044715
+f32 = jnp.float32
+bf16 = jnp.bfloat16
+AXES = ("dp", "mp")
+GRID = (4, 2, 2, 2)
 
 
 def gelu_pair(pre_act):
@@ -20,7 +27,13 @@
     return (gelu_value, gelu_slope)
 
 
-def local(
+def token_advantage(teacher_ids, adv_table):
+    classes = adv_table.shape[0]
+    class_hit = teacher_ids[:, None] == jnp.arange(classes, dtype=jnp.int32)[None, :]
+    return jnp.sum(jnp.where(class_hit, adv_table[None, :], 0.0), axis=1)
+
+
+def local_any(
     layer_input,
     gate_pre,
     up_pre,
@@ -37,35 +50,29 @@
     block_rows = gate_weight.shape[0]
     block_cols = gate_weight.shape[1]
     token_count = layer_input.shape[0]
-    classes = adv_table.shape[0]
-    class_hit = teacher_ids[:, None] == jnp.arange(classes, dtype=jnp.int32)[None, :]
-    advantage = jnp.sum(jnp.where(class_hit, adv_table[None, :], 0.0), axis=1)
-    weighted = hidden_cot.astype(jnp.float32) * advantage[:, None]
-    gelu_value, gelu_slope = gelu_pair(gate_pre.astype(jnp.float32))
-    gate_grad = (weighted * up_pre.astype(jnp.float32) * gelu_slope).astype(jnp.bfloat16)
-    up_grad = (weighted * gelu_value).astype(jnp.bfloat16)
+    advantage = token_advantage(teacher_ids, adv_table)
+    weighted = hidden_cot.astype(f32) * advantage[:, None]
+    gelu_value, gelu_slope = gelu_pair(gate_pre.astype(f32))
+    gate_grad = (weighted * up_pre.astype(f32) * gelu_slope).astype(bf16)
+    up_grad = (weighted * gelu_value).astype(bf16)
     contract_last = (((1,), (1,)), ((), ()))
     contract_first = (((0,), (0,)), ((), ()))
     pieces = lax.all_gather((gate_weight, up_weight), "dp", axis=0, tiled=True)
     partial_sum = lax.dot_general(
-        gate_grad, pieces[0], contract_last, preferred_element_type=jnp.float32
-    ) + lax.dot_general(up_grad, pieces[1], contract_last, preferred_element_type=jnp.float32)
+        gate_grad, pieces[0], contract_last, preferred_element_type=f32
+    ) + lax.dot_general(up_grad, pieces[1], contract_last, preferred_element_type=f32)
     input_grad = lax.psum_scatter(
-        partial_sum.astype(jnp.bfloat16), "mp", scatter_dimension=1, tiled=True
+        partial_sum.astype(bf16), "mp", scatter_dimension=1, tiled=True
     )
     grad_scale = 1.0 / math.sqrt(token_count * data_size)
-    gate_term = lax.dot_general(
-        layer_input, gate_grad, contract_first, preferred_element_type=jnp.float32
-    )
-    up_term = lax.dot_general(
-        layer_input, up_grad, contract_first, preferred_element_type=jnp.float32
-    )
+    gate_term = lax.dot_general(layer_input, gate_grad, contract_first, preferred_element_type=f32)
+    up_term = lax.dot_general(layer_input, up_grad, contract_first, preferred_element_type=f32)
     summed = lax.psum_scatter(
-        jnp.concatenate([gate_term, up_term], axis=1).astype(jnp.bfloat16),
+        jnp.concatenate([gate_term, up_term], axis=1).astype(bf16),
         "dp",
         scatter_dimension=0,
         tiled=True,
-    ).astype(jnp.float32)
+    ).astype(f32)
     grad_gate = summed[:, :block_cols] * grad_scale
     grad_up = summed[:, block_cols:] * grad_scale
     squares_gate = grad_gate * grad_gate
@@ -93,6 +100,216 @@
     return (input_grad, gate_update, up_update, new_rows, new_cols)
 
 
+def device_number(place):
+    number = 0
+    for coordinate, size in zip(place, GRID):
+        number = number * size + coordinate
+    return number
+
+
+def pairs(target):
+    out = []
+    for z in range(GRID[0]):
+        for x in range(GRID[1]):
+            for y in range(GRID[2]):
+                for c in range(GRID[3]):
+                    place = target(z, x, y, c)
+                    if place is not None:
+                        out.append((device_number((z, x, y, c)), device_number(place)))
+    return out
+
+
+def flip_z(k):
+    return pairs(lambda z, x, y, c: (z ^ k, x, y, c))
+
+
+FLIP_X = pairs(lambda z, x, y, c: (z, 1 - x, y, c))
+FLIP_Y = pairs(lambda z, x, y, c: (z, x, 1 - y, c))
+FLIP_C = pairs(lambda z, x, y, c: (z, x, y, 1 - c))
+MIDDLE = pairs(lambda z, x, y, c: (3 - z, x, y, c) if z in (1, 2) else None)
+OUTWARD = pairs(lambda z, x, y, c: ({1: 0, 2: 3}[z], x, y, c) if z in (1, 2) else None)
+HOME = pairs(lambda z, x, y, c: (z ^ (2 * y + c), x, z >> 1, z & 1))
+
+
+def send(value, permutation):
+    return lax.ppermute(value, AXES, permutation)
+
+
+def front_kernel(ids_ref, table_ref, cot_ref, gate_ref, up_ref, gate_out, up_out):
+    classes = table_ref.shape[1]
+    ids = ids_ref[...]
+    hit = ids == lax.broadcasted_iota(jnp.int32, (ids.shape[0], classes), 1)
+    advantage = jnp.sum(jnp.where(hit, table_ref[...], 0.0), axis=1, keepdims=True)
+    weighted = cot_ref[...].astype(f32) * advantage
+    value, slope = gelu_pair(gate_ref[...].astype(f32))
+    gate_out[...] = (weighted * up_ref[...].astype(f32) * slope).astype(bf16)
+    up_out[...] = (weighted * value).astype(bf16)
+
+
+def front(teacher_ids, adv_table, hidden_cot, gate_pre, up_pre, start, width):
+    tokens = hidden_cot.shape[0]
+    rows = 128
+    first = start // width
+    block = pl.BlockSpec((rows, width), lambda i: (i, first))
+    out_block = pl.BlockSpec((rows, width), lambda i: (i, 0))
+    shape = jax.ShapeDtypeStruct((tokens, width), bf16)
+    return pl.pallas_call(
+        front_kernel,
+        grid=(tokens // rows,),
+        in_specs=[
+            pl.BlockSpec((rows, 1), lambda i: (i, 0)),
+            pl.BlockSpec((1, adv_table.shape[0]), lambda i: (0, 0)),
+            block,
+            block,
+            block,
+        ],
+        out_specs=[out_block, out_block],
+        out_shape=[shape, shape],
+        cost_estimate=pl.CostEstimate(
+            flops=60 * tokens * width, bytes_accessed=10 * tokens * width, transcendentals=0
+        ),
+    )(teacher_ids[:, None], adv_table[None, :], hidden_cot, gate_pre, up_pre)
+
+
+def gather_column(own):
+    near = send(own, flip_z(1))
+    across_own = send(own, MIDDLE)
+    across_near = send(near, MIDDLE)
+    out_own = send(across_own, OUTWARD)
+    out_near = send(across_near, OUTWARD)
+    return jnp.concatenate([own, near, across_near + out_own, across_own + out_near], axis=0)
+
+
+def dot_first(a, b):
+    return lax.dot_general(a, b, (((0,), (0,)), ((), ())), preferred_element_type=f32)
+
+
+def dot_last(a, b):
+    return lax.dot_general(a, b, (((1,), (1,)), ((), ())), preferred_element_type=f32)
+
+
+def sum_over(value, permutations):
+    for permutation in permutations:
+        value = value + send(value, permutation)
+    return value
+
+
+OVER_DP = (FLIP_X, flip_z(1), flip_z(2))
+OVER_MP = (FLIP_C, FLIP_Y)
+
+
+def local_block(
+    layer_input,
+    gate_pre,
+    up_pre,
+    hidden_cot,
+    teacher_ids,
+    adv_table,
+    gate_weight,
+    up_weight,
+    row_moments,
+    col_moments,
+):
+    data_size = lax.axis_size("dp")
+    model_size = lax.axis_size("mp")
+    rows, cols = gate_weight.shape
+    tokens = layer_input.shape[0]
+    dp = lax.axis_index("dp")
+    m = lax.axis_index("mp")
+    z, x = dp // 2, dp % 2
+    y, c = m // 2, m % 2
+    piece_rows = tokens // model_size
+    plane = 2 * rows
+
+    def input_columns(array, k):
+        base = (z ^ k) * plane
+        size = array.shape[0]
+        return jnp.concatenate(
+            [
+                lax.dynamic_slice(array, (0, base + x * rows), (size, rows)),
+                lax.dynamic_slice(array, (0, base + (1 - x) * rows), (size, rows)),
+            ],
+            axis=1,
+        )
+
+    mine = lax.dynamic_slice(layer_input, (m * piece_rows, 0), (piece_rows, layer_input.shape[1]))
+    piece = jnp.stack([send(input_columns(mine, k), flip_z(k)) for k in (1, 2, 3)])
+    piece_c = send(piece, FLIP_C)
+    piece_y = send(piece, FLIP_Y)
+    piece_yc = send(piece_y, FLIP_C)
+    far = jnp.zeros((3, model_size, piece_rows, plane), bf16)
+    for part, place in ((piece, m), (piece_c, m ^ 1), (piece_y, m ^ 2), (piece_yc, m ^ 3)):
+        far = lax.dynamic_update_slice(far, part[:, None], (0, place, 0, 0))
+    inputs = jnp.concatenate(
+        [input_columns(layer_input, 0), far.reshape(3 * tokens, plane)], axis=0
+    )
+
+    def plane_rows(weight):
+        other = send(weight, FLIP_X)
+        both = jnp.zeros((plane, cols), bf16)
+        both = lax.dynamic_update_slice(both, weight, (x * rows, 0))
+        return lax.dynamic_update_slice(both, other, ((1 - x) * rows, 0))
+
+    weights = (plane_rows(gate_weight), plane_rows(up_weight))
+
+    width = cols // 2
+    grads = [
+        front(teacher_ids, adv_table, hidden_cot, gate_pre, up_pre, start, width)
+        for start in range(0, cols, width)
+    ]
+    grad_scale = 1.0 / math.sqrt(tokens * data_size)
+    partial_input = None
+    sums = []
+    for k in range(2):
+        chunks = []
+        for position, start in enumerate(range(0, cols, width)):
+            gathered = gather_column(grads[position][k])
+            away = dot_first(inputs[:, rows:], gathered).astype(bf16)
+            keep = dot_first(inputs[:, :rows], gathered)
+            chunks.append((keep + send(away, FLIP_X).astype(f32)) * grad_scale)
+            term = dot_last(gathered, weights[k][:, start : start + width])
+            partial_input = term if partial_input is None else partial_input + term
+        sums.append(chunks)
+
+    blocks = partial_input.reshape(2, 2, tokens, plane)
+    keep = jnp.where(c == 0, blocks[:, 0], blocks[:, 1])
+    away = jnp.where(c == 0, blocks[:, 1], blocks[:, 0]).astype(bf16)
+    blocks = keep + send(away, FLIP_C).astype(f32)
+    keep = jnp.where(y == 0, blocks[0], blocks[1])
+    away = jnp.where(y == 0, blocks[1], blocks[0]).astype(bf16)
+    block = (keep + send(away, FLIP_Y).astype(f32)).astype(bf16)
+    input_grad = send(block, HOME)
+
+    entry_count = rows * data_size * cols * model_size
+    updates, new_rows, new_cols = [], [], []
+    for k, chunks in enumerate(sums):
+        squares = [chunk * chunk for chunk in chunks]
+        row_total = sum_over(sum(jnp.sum(s, axis=1) for s in squares), OVER_MP)
+        row = decay_rate * row_moments[k] + (1.0 - decay_rate) * (
+            row_total / (cols * model_size)
+        )
+        col_total = sum_over(
+            jnp.concatenate([jnp.sum(s, axis=0) for s in squares]), OVER_DP
+        )
+        col = decay_rate * col_moments[k] + (1.0 - decay_rate) * (
+            col_total / (rows * data_size)
+        )
+        row_factor = lax.rsqrt(row)[:, None]
+        col_factor = lax.rsqrt(col)[None, :]
+        scaled = [
+            chunk * row_factor * col_factor[:, i * width : (i + 1) * width]
+            for i, chunk in enumerate(chunks)
+        ]
+        square_sum = sum_over(
+            jnp.broadcast_to(sum(jnp.sum(s * s) for s in scaled), (128,)), OVER_MP + OVER_DP
+        )[0]
+        factor = lax.rsqrt(square_sum / entry_count + 1e-06)
+        updates.append(jnp.concatenate([s * factor for s in scaled], axis=1))
+        new_rows.append(row)
+        new_cols.append(col)
+    return (input_grad, updates[0], updates[1], jnp.stack(new_rows), jnp.stack(new_cols))
+
+
 def solution(mesh):
     in_specs = (
         P("dp", None),
@@ -107,4 +324,6 @@
         P(None, "mp"),
     )
     out_specs = (P("dp", "mp"), P("dp", "mp"), P("dp", "mp"), P(None, "dp"), P(None, "mp"))
+    fits = (mesh.shape["dp"], mesh.shape["mp"]) == (GRID[0] * GRID[1], GRID[2] * GRID[3])
+    local = local_block if fits else local_any
     return jax.shard_map(local, mesh=mesh, in_specs=in_specs, out_specs=out_specs, check_vma=False)

time: 769 us -> 417 us (0.54)
  the two profiles are of different devices: /device:TPU:1 before, /device:TPU:4 now
where the time goes in v1:
time: 417 us; the launch traced here: 409 us
  waiting for transfers between devices  196 us (47%)
  starting transfers between devices  87.4 us (21%)
  matrix products  68.1 us (16%)
  other arithmetic  27.5 us (7%)
  local copies, waits for them, and re-layouts  16.4 us (4%)
  Pallas kernels  8.76 us (2%)
  between operations  4.94 us (1%)
    ppermute x55, waiting for transfers between devices, send(): return lax.ppermute(value, AXES, permutation)  196 us
    ppermute x55, starting transfers between devices, send(): return lax.ppermute(value, AXES, permutation)  87.4 us
    dot_general x4, matrix products, dot_last(): lax.dot_general(a, b, (((1,), (1,)), ((), ())), preferred_element_type=f32)  37.5 us
    dot_general x8, matrix products, dot_first(): lax.dot_general(a, b, (((0,), (0,)), ((), ())), preferred_element_type=f32)  30.6 us
    pallas_call x2, Pallas kernels, front(): pl.pallas_call(front_kernel, grid=(tokens // rows,), in_specs=[pl.BlockSp...  8.76 us
  transfers between devices with their start and end apart: 55, of which 22 were waited for; matrix products, arithmetic and copies ran while one was open for 25% of the time, Pallas kernels for 1%

profile of v1, /device:TPU:4, one launch (start us, length us, event | category | flops | bytes accessed | tf_op | source)
XLA Modules:
  0.0 409.4 jit_solution(649459458958182525)
XLA Ops:
  2.2 4.4 %shard_map.138 = (bf16[512,640]{1,0:T(8,128)(2,1)}, bf16[512,640]{1,0:T(8,128)(2,1)}) custom-call(s32[512,1]{1,0:T(8,128)} %copy.17.ids_ref, f32[1,64]{1,0:T(1,128)} %bitcast.69, bf16[512,1280]{1,0:T(8,128)(2,1)} %cot_ref.3, bf16[512,1280]{1,0:T(8,128)(2,1)} %gate_ref.3, bf16[512,1280]{1,0:T(8,128)(2,1)} %up_ref.3), custom_call_target="tpu_custom_call" | custom-call | flops 19660800 | bytes 3276800 | tf_op jit(solution)/shard_map/pallas_call | solution.py:156
  8.1 3.6 collective-permute-start.6
  18.3 16.2 %collective-permute-done.27 = bf16[128,1024]{1,0:T(8,128)(2,1)S(1)} collective-permute-done((bf16[128,1024]{1,0:T(8,128)(2,1)S(1)}, bf16[128,1024]{1,0:T(8,128)(2,1)S(1)}, u32[]{:S(2)}, u32[]{:S(2)}) %collective-permute-start.27) | collective-permute-done | bytes 262176 | tf_op jit(solution)/shard_map/ppermute | solution.py:135
  34.6 24.2 %collective-permute-start.25 = (bf16[128,1024]{1,0:T(8,128)(2,1)S(1)}, bf16[128,1024]{1,0:T(8,128)(2,1)S(1)}, u32[]{:S(2)}, u32[]{:S(2)}) collective-permute-start(bf16[128,1024]{1,0:T(8,128)(2,1)S(1)} %pad_maximum_fusion.8), channel_id=1, source_target_pairs={{0,8},{1,9},{2,10},{3,11},{4,12},{5,13},{6,14},{7,15},{8,0},{9,1},... | collective-permute-start | bytes 786440 | tf_op jit(solution)/shard_map/ppermute | solution.py:135
  58.7 4.0 collective-permute-done.26
  62.8 4.4 %shard_map.137 = (bf16[512,640]{1,0:T(8,128)(2,1)}, bf16[512,640]{1,0:T(8,128)(2,1)}) custom-call(s32[512,1]{1,0:T(8,128)} %copy.17.ids_ref, f32[1,64]{1,0:T(1,128)} %bitcast.70, bf16[512,1280]{1,0:T(8,128)(2,1)} %cot_ref.3, bf16[512,1280]{1,0:T(8,128)(2,1)} %gate_ref.3, bf16[512,1280]{1,0:T(8,128)(2,1)} %up_ref.3), custom_call_target="tpu_custom_call" | custom-call | flops 19660800 | bytes 3276800 | tf_op jit(solution)/shard_map/pallas_call | solution.py:156
  76.5 6.1 %collective-permute-done.17 = bf16[512,640]{1,0:T(8,128)(2,1)} collective-permute-done((bf16[512,640]{1,0:T(8,128)(2,1)}, bf16[512,640]{1,0:T(8,128)(2,1)}, u32[]{:S(2)}, u32[]{:S(2)}) %collective-permute-start.17) | collective-permute-done | bytes 655392 | tf_op jit(solution)/shard_map/ppermute | solution.py:135
  83.1 13.5 %collective-permute-done = bf16[512,640]{1,0:T(8,128)(2,1)} collective-permute-done((bf16[512,640]{1,0:T(8,128)(2,1)}, bf16[512,640]{1,0:T(8,128)(2,1)}, u32[]{:S(2)}, u32[]{:S(2)}) %collective-permute-start) | collective-permute-done | bytes 655392 | tf_op jit(solution)/shard_map/ppermute | solution.py:135
  99.4 11.3 %collective-permute-done.11 = bf16[512,640]{1,0:T(8,128)(2,1)} collective-permute-done((bf16[512,640]{1,0:T(8,128)(2,1)}, bf16[512,640]{1,0:T(8,128)(2,1)}, u32[]{:S(2)}, u32[]{:S(2)}) %collective-permute-start.11) | collective-permute-done | bytes 655392 | tf_op jit(solution)/shard_map/ppermute | solution.py:135
  117.7 7.0 %collective-permute-done.9 = bf16[512,640]{1,0:T(8,128)(2,1)} collective-permute-done((bf16[512,640]{1,0:T(8,128)(2,1)}, bf16[512,640]{1,0:T(8,128)(2,1)}, u32[]{:S(2)}, u32[]{:S(2)}) %collective-permute-start.9) | collective-permute-done | bytes 655392 | tf_op jit(solution)/shard_map/ppermute | solution.py:135
  128.7 9.9 %collective-permute-done.20 = bf16[512,640]{1,0:T(8,128)(2,1)S(1)} collective-permute-done((bf16[512,640]{1,0:T(8,128)(2,1)S(1)}, bf16[512,640]{1,0:T(8,128)(2,1)S(1)}, u32[]{:S(2)}, u32[]{:S(2)}) %collective-permute-start.20) | collective-permute-done | bytes 655392 | tf_op jit(solution)/shard_map/ppermute | solution.py:135
  139.4 12.8 %collective-permute-done.3 = bf16[512,640]{1,0:T(8,128)(2,1)S(1)} collective-permute-done((bf16[512,640]{1,0:T(8,128)(2,1)}, bf16[512,640]{1,0:T(8,128)(2,1)S(1)}, u32[]{:S(2)}, u32[]{:S(2)}) %collective-permute-start.3) | collective-permute-done | bytes 655392 | tf_op jit(solution)/shard_map/ppermute | solution.py:135
  161.7 10.2 %collective-permute-done.14 = bf16[512,640]{1,0:T(8,128)(2,1)S(1)} collective-permute-done((bf16[512,640]{1,0:T(8,128)(2,1)}, bf16[512,640]{1,0:T(8,128)(2,1)S(1)}, u32[]{:S(2)}, u32[]{:S(2)}) %collective-permute-start.14) | collective-permute-done | bytes 655392 | tf_op jit(solution)/shard_map/ppermute | solution.py:135
  174.8 4.3 %pad_maximum_fusion = bf16[2048,1024]{1,0:T(8,128)(2,1)S(1)} fusion(bf16[1536,1024]{1,0:T(8,128)(2,1)S(1)} %bitcast.57, bf16[512,512]{1,0:T(8,128)(2,1)S(1)} %get-tuple-element.40, bf16[512,512]{1,0:T(8,128)(2,1)S(1)} %get-tuple-element.39), kind=kLoop, calls=%fused_computation.3 | loop fusion | flops 12582912 | bytes 8388608 | tf_op jit(solution)/shard_map/concatenate | solution.py:243
  179.1 6.8 %collective-permute-done.4 = bf16[512,640]{1,0:T(8,128)(2,1)S(1)} collective-permute-done((bf16[512,640]{1,0:T(8,128)(2,1)S(1)}, bf16[512,640]{1,0:T(8,128)(2,1)S(1)}, u32[]{:S(2)}, u32[]{:S(2)}) %collective-permute-start.4) | collective-permute-done | bytes 655392 | tf_op jit(solution)/shard_map/ppermute | solution.py:135
  187.2 4.0 fusion.14
  192.7 21.3 %collective-permute-done.21 = bf16[512,640]{1,0:T(8,128)(2,1)S(1)} collective-permute-done((bf16[512,640]{1,0:T(8,128)(2,1)S(1)}, bf16[512,640]{1,0:T(8,128)(2,1)S(1)}, u32[]{:S(2)}, u32[]{:S(2)}) %collective-permute-start.21) | collective-permute-done | bytes 655392 | tf_op jit(solution)/shard_map/ppermute | solution.py:135
  214.2 4.3 %fusion.23 = bf16[512,640]{1,0:T(8,128)(2,1)} fusion(bf16[2048,1024]{1,0:T(8,128)(2,1)S(1)} %pad_maximum_fusion, bf16[512,640]{1,0:T(8,128)(2,1)S(1)} %add.248, bf16[512,640]{1,0:T(8,128)(2,1)S(1)} %add.247, bf16[512,640]{1,0:T(8,128)(2,1)} %collective-permute-done.17, bf16[512,640]{1,0:T(8,128)(2,1)} %get-tuple-element.12), kind=kOutput, calls=%fused_computation.35 | convolution fusion | flops 1352990720 | bytes 5373952 | tf_op jit(solution)/shard_map/dot_general | solution.py:184
  220.0 6.6 %collective-permute-done.15 = bf16[512,640]{1,0:T(8,128)(2,1)S(1)} collective-permute-done((bf16[512,640]{1,0:T(8,128)(2,1)S(1)}, bf16[512,640]{1,0:T(8,128)(2,1)S(1)}, u32[]{:S(2)}, u32[]{:S(2)}) %collective-permute-start.15) | collective-permute-done | bytes 655392 | tf_op jit(solution)/shard_map/ppermute | solution.py:135
  227.9 4.1 fusion.20
  234.8 4.1 fusion.17
  239.4 8.0 %fusion.32 = f32[2048,1024]{1,0:T(8,128)} fusion(bf16[1024,1280]{1,0:T(8,128)(2,1)S(1)} %constant_dynamic-update-slice_fusion.2, bf16[512,640]{1,0:T(8,128)(2,1)S(1)} %add.242, bf16[512,640]{1,0:T(8,128)(2,1)S(1)} %add.241, bf16[512,640]{1,0:T(8,128)(2,1)} %collective-permute-done.6, bf16[512,640]{1,0:T(8,128)(2,1)S(1)} %copy-done.30), kind=kOutput, calls=%fused_computation.40 | convolution fusion | flops 2694840320 | bytes 12320768 | tf_op jit(solution)/shard_map/dot_general | solution.py:188
  247.4 8.2 %fusion.34 = f32[2048,1024]{1,0:T(8,128)} fusion(bf16[1024,1280]{1,0:T(8,128)(2,1)S(1)} %constant_dynamic-update-slice_fusion.2, bf16[512,640]{1,0:T(8,128)(2,1)S(1)} %add.237, bf16[512,640]{1,0:T(8,128)(2,1)S(1)} %add.236, bf16[512,640]{1,0:T(8,128)(2,1)} %collective-permute-done, bf16[512,640]{1,0:T(8,128)(2,1)S(1)} %copy-done.32), kind=kOutput, calls=%fused_computation.42 | convolution fusion | flops 2694840320 | bytes 12320768 | tf_op jit(solution)/shard_map/dot_general | solution.py:188
  255.6 8.0 %fusion.30 = f32[2048,1024]{1,0:T(8,128)} fusion(bf16[1024,1280]{1,0:T(8,128)(2,1)S(1)} %constant_dynamic-update-slice_fusion, bf16[512,640]{1,0:T(8,128)(2,1)S(1)} %add.245, bf16[512,640]{1,0:T(8,128)(2,1)S(1)} %add.244, bf16[512,640]{1,0:T(8,128)(2,1)} %collective-permute-done.11, bf16[512,640]{1,0:T(8,128)(2,1)S(1)} %copy-done.34), kind=kOutput, calls=%fused_computation.38 | convolution fusion | flops 2694840320 | bytes 12320768 | tf_op jit(solution)/shard_map/dot_general | solution.py:188
  263.6 13.4 %add_add_fusion = f32[2048,1024]{1,0:T(8,128)S(1)} fusion(f32[2048,1024]{1,0:T(8,128)} %fusion.30, f32[2048,1024]{1,0:T(8,128)} %fusion.34, f32[2048,1024]{1,0:T(8,128)} %fusion.32, bf16[1024,1280]{1,0:T(8,128)(2,1)} %copy-done.1, bf16[512,640]{1,0:T(8,128)(2,1)S(1)} %add.248, bf16[512,640]{1,0:T(8,128)(2,1)S(1)} %add.247, ...), kind=kOutput, calls=%fused_computation | convolution fusion | flops 2701131776 | bytes 37486592 | tf_op jit(solution)/shard_map/dot_general | solution.py:188
  278.7 3.5 copy-done.7
  291.9 3.6 fusion.37
  295.5 3.7 fusion.39
  317.2 5.7 %bitcast_add_fusion = f32[2,512,1024]{2,1,0:T(8,128)S(1)} fusion(bf16[2,512,1024]{2,1,0:T(8,128)(2,1)} %collective-permute-done.22, f32[2,2,512,1024]{3,2,1,0:T(8,128)} %bitcast.56, pred[]{:T(512)S(6)} %eq.12), kind=kLoop, calls=%fused_computation.4 | loop fusion | flops 3145728 | bytes 14680065 | tf_op jit(solution)/shard_map/add | solution.py:277
  325.7 22.6 %collective-permute-done.39 = f32[128]{0:T(128)S(1)} collective-permute-done((f32[128]{0:T(128)S(1)}, f32[128]{0:T(128)S(1)}, u32[]{:S(2)}, u32[]{:S(2)}) %collective-permute-start.39) | collective-permute-done | bytes 544 | tf_op jit(solution)/shard_map/ppermute | solution.py:135
  360.6 4.1 collective-permute-start.24
  368.9 39.1 %collective-permute-done.24 = bf16[512,1024]{1,0:T(8,128)(2,1)S(1)} collective-permute-done((bf16[512,1024]{1,0:T(8,128)(2,1)S(1)}, bf16[512,1024]{1,0:T(8,128)(2,1)S(1)}, u32[]{:S(2)}, u32[]{:S(2)}) %collective-permute-start.24) | collective-permute-done | bytes 1048608 | tf_op jit(solution)/shard_map/ppermute | solution.py:135
  (237 shorter events, 101.6 us)
Async XLA Ops:
  6.6 63.4 %collective-permute-start.8 = (bf16[512,640]{1,0:T(8,128)(2,1)}, bf16[512,640]{1,0:T(8,128)(2,1)}, u32[]{:S(2)}, u32[]{:S(2)}) collective-permute-start(bf16[512,640]{1,0:T(8,128)(2,1)} %get-tuple-element.10), channel_id=1, source_target_pairs={{8,16},{9,17},{10,18},{11,19},{12,20},{13,21},{14,22},{15,23},{16,... | collective-permute-start | bytes 1966088 | tf_op jit(solution)/shard_map/ppermute | solution.py:135
  8.1 64.7 %collective-permute-start.6 = (bf16[512,640]{1,0:T(8,128)(2,1)}, bf16[512,640]{1,0:T(8,128)(2,1)}, u32[]{:S(2)}, u32[]{:S(2)}) collective-permute-start(bf16[512,640]{1,0:T(8,128)(2,1)} %get-tuple-element.10), channel_id=1, source_target_pairs={{0,8},{1,9},{2,10},{3,11},{4,12},{5,13},{6,14},{7,15},{8,0},{9,1},... | collective-permute-start | bytes 1966088 | tf_op jit(solution)/shard_map/ppermute | solution.py:135
  11.7 62.6 %collective-permute-start.19 = (bf16[512,640]{1,0:T(8,128)(2,1)}, bf16[512,640]{1,0:T(8,128)(2,1)S(1)}, u32[]{:S(2)}, u32[]{:S(2)}) collective-permute-start(bf16[512,640]{1,0:T(8,128)(2,1)} %get-tuple-element.12), channel_id=1, source_target_pairs={{8,16},{9,17},{10,18},{11,19},{12,20},{13,21},{14,22},{15,23},{16,... | collective-permute-start | bytes 1966088 | tf_op jit(solution)/shard_map/ppermute | solution.py:135
  14.4 20.2 %collective-permute-start.27 = (bf16[128,1024]{1,0:T(8,128)(2,1)S(1)}, bf16[128,1024]{1,0:T(8,128)(2,1)S(1)}, u32[]{:S(2)}, u32[]{:S(2)}) collective-permute-start(bf16[128,1024]{1,0:T(8,128)(2,1)S(1)} %pad_maximum_fusion.10), channel_id=1, source_target_pairs={{0,24},{1,25},{2,26},{3,27},{4,28},{5,29},{6,30},{7,31},{8,16},{9,... | collective-permute-start | bytes 786440 | tf_op jit(solution)/shard_map/ppermute | solution.py:135
  15.8 46.9 %collective-permute-start.26 = (bf16[128,1024]{1,0:T(8,128)(2,1)S(1)}, bf16[128,1024]{1,0:T(8,128)(2,1)S(1)}, u32[]{:S(2)}, u32[]{:S(2)}) collective-permute-start(bf16[128,1024]{1,0:T(8,128)(2,1)S(1)} %pad_maximum_fusion.9), channel_id=1, source_target_pairs={{0,16},{1,17},{2,18},{3,19},{4,20},{5,21},{6,22},{7,23},{8,24},{9,... | collective-permute-start | bytes 786440 | tf_op jit(solution)/shard_map/ppermute | solution.py:135
  34.6 33.8 %collective-permute-start.25 = (bf16[128,1024]{1,0:T(8,128)(2,1)S(1)}, bf16[128,1024]{1,0:T(8,128)(2,1)S(1)}, u32[]{:S(2)}, u32[]{:S(2)}) collective-permute-start(bf16[128,1024]{1,0:T(8,128)(2,1)S(1)} %pad_maximum_fusion.8), channel_id=1, source_target_pairs={{0,8},{1,9},{2,10},{3,11},{4,12},{5,13},{6,14},{7,15},{8,0},{9,1},... | collective-permute-start | bytes 786440 | tf_op jit(solution)/shard_map/ppermute | solution.py:135
  69.9 26.7 %collective-permute-start = (bf16[512,640]{1,0:T(8,128)(2,1)}, bf16[512,640]{1,0:T(8,128)(2,1)}, u32[]{:S(2)}, u32[]{:S(2)}) collective-permute-start(bf16[512,640]{1,0:T(8,128)(2,1)} %get-tuple-element.9), channel_id=1, source_target_pairs={{0,8},{1,9},{2,10},{3,11},{4,12},{5,13},{6,14},{7,15},{8,0},{9,1},... | collective-permute-start | bytes 1966088 | tf_op jit(solution)/shard_map/ppermute | solution.py:135
  72.7 25.4 %collective-permute-start.13 = (bf16[512,640]{1,0:T(8,128)(2,1)}, bf16[512,640]{1,0:T(8,128)(2,1)}, u32[]{:S(2)}, u32[]{:S(2)}) collective-permute-start(bf16[512,640]{1,0:T(8,128)(2,1)} %get-tuple-element.11), channel_id=1, source_target_pairs={{8,16},{9,17},{10,18},{11,19},{12,20},{13,21},{14,22},{15,23},{16,... | collective-permute-start | bytes 1966088 | tf_op jit(solution)/shard_map/ppermute | solution.py:135
  74.2 36.4 %collective-permute-start.11 = (bf16[512,640]{1,0:T(8,128)(2,1)}, bf16[512,640]{1,0:T(8,128)(2,1)}, u32[]{:S(2)}, u32[]{:S(2)}) collective-permute-start(bf16[512,640]{1,0:T(8,128)(2,1)} %get-tuple-element.11), channel_id=1, source_target_pairs={{0,8},{1,9},{2,10},{3,11},{4,12},{5,13},{6,14},{7,15},{8,0},{9,1},... | collective-permute-start | bytes 1966088 | tf_op jit(solution)/shard_map/ppermute | solution.py:135
  82.6 31.3 %collective-permute-start.28 = (bf16[3,128,1024]{2,1,0:T(8,128)(2,1)}, bf16[3,128,1024]{2,1,0:T(8,128)(2,1)}, u32[]{:S(2)}, u32[]{:S(2)}) collective-permute-start(bf16[3,128,1024]{2,1,0:T(8,128)(2,1)} %pad_maximum_fusion.7), channel_id=1, source_target_pairs={{0,1},{1,0},{2,3},{3,2},{4,5},{5,4},{6,7},{7,6},{8,9},{9,8},{10,11... | collective-permute-start | bytes 2359304 | tf_op jit(solution)/shard_map/ppermute | solution.py:135
  82.6 33.8 %collective-permute-start.29 = (bf16[3,128,1024]{2,1,0:T(8,128)(2,1)}, bf16[3,128,1024]{2,1,0:T(8,128)(2,1)}, u32[]{:S(2)}, u32[]{:S(2)}) collective-permute-start(bf16[3,128,1024]{2,1,0:T(8,128)(2,1)} %pad_maximum_fusion.7), channel_id=1, source_target_pairs={{0,2},{1,3},{2,0},{3,1},{4,6},{5,7},{6,4},{7,5},{8,10},{9,11},{10,... | collective-permute-start | bytes 2359304 | tf_op jit(solution)/shard_map/ppermute | solution.py:135
  96.6 57.5 %collective-permute-start.16 = (bf16[512,1280]{1,0:T(8,128)(2,1)S(1)}, bf16[512,1280]{1,0:T(8,128)(2,1)}, u32[]{:S(2)}, u32[]{:S(2)}) collective-permute-start(bf16[512,1280]{1,0:T(8,128)(2,1)S(1)} %copy-done.12), channel_id=1, source_target_pairs={{0,4},{1,5},{2,6},{3,7},{4,0},{5,1},{6,2},{7,3},{8,12},{9,13},{10,... | collective-permute-start | bytes 3932168 | tf_op jit(solution)/shard_map/ppermute | solution.py:135
  98.1 26.6 %collective-permute-start.9 = (bf16[512,640]{1,0:T(8,128)(2,1)}, bf16[512,640]{1,0:T(8,128)(2,1)}, u32[]{:S(2)}, u32[]{:S(2)}) collective-permute-start(bf16[512,640]{1,0:T(8,128)(2,1)} %collective-permute-done.8), channel_id=1, source_target_pairs={{8,0},{9,1},{10,2},{11,3},{12,4},{13,5},{14,6},{15,7},{16,24},{17,... | collective-permute-start | bytes 1966088 | tf_op jit(solution)/shard_map/ppermute | solution.py:135
  114.8 42.1 %collective-permute-start.5 = (bf16[512,1280]{1,0:T(8,128)(2,1)S(1)}, bf16[512,1280]{1,0:T(8,128)(2,1)S(1)}, u32[]{:S(2)}, u32[]{:S(2)}) collective-permute-start(bf16[512,1280]{1,0:T(8,128)(2,1)S(1)} %copy-done.13), channel_id=1, source_target_pairs={{0,4},{1,5},{2,6},{3,7},{4,0},{5,1},{6,2},{7,3},{8,12},{9,13},{10,... | collective-permute-start | bytes 3932168 | tf_op jit(solution)/shard_map/ppermute | solution.py:135
  116.4 22.3 %collective-permute-start.20 = (bf16[512,640]{1,0:T(8,128)(2,1)S(1)}, bf16[512,640]{1,0:T(8,128)(2,1)S(1)}, u32[]{:S(2)}, u32[]{:S(2)}) collective-permute-start(bf16[512,640]{1,0:T(8,128)(2,1)S(1)} %copy-done.15), channel_id=1, source_target_pairs={{8,0},{9,1},{10,2},{11,3},{12,4},{13,5},{14,6},{15,7},{16,24},{17,... | collective-permute-start | bytes 1966088 | tf_op jit(solution)/shard_map/ppermute | solution.py:135
  124.7 27.4 %collective-permute-start.3 = (bf16[512,640]{1,0:T(8,128)(2,1)}, bf16[512,640]{1,0:T(8,128)(2,1)S(1)}, u32[]{:S(2)}, u32[]{:S(2)}) collective-permute-start(bf16[512,640]{1,0:T(8,128)(2,1)} %collective-permute-done.2), channel_id=1, source_target_pairs={{8,0},{9,1},{10,2},{11,3},{12,4},{13,5},{14,6},{15,7},{16,24},{17,... | collective-permute-start | bytes 1966088 | tf_op jit(solution)/shard_map/ppermute | solution.py:135
  126.0 27.4 %collective-permute-start.1 = (bf16[512,640]{1,0:T(8,128)(2,1)}, bf16[512,640]{1,0:T(8,128)(2,1)S(1)}, u32[]{:S(2)}, u32[]{:S(2)}) collective-permute-start(bf16[512,640]{1,0:T(8,128)(2,1)} %collective-permute-done), channel_id=1, source_target_pairs={{8,16},{9,17},{10,18},{11,19},{12,20},{13,21},{14,22},{15,23},{16,... | collective-permute-start | bytes 1966088 | tf_op jit(solution)/shard_map/ppermute | solution.py:135
  138.7 21.6 %collective-permute-start.18 = (bf16[512,640]{1,0:T(8,128)(2,1)}, bf16[512,640]{1,0:T(8,128)(2,1)S(1)}, u32[]{:S(2)}, u32[]{:S(2)}) collective-permute-start(bf16[512,640]{1,0:T(8,128)(2,1)} %collective-permute-done.17), channel_id=1, source_target_pairs={{8,16},{9,17},{10,18},{11,19},{12,20},{13,21},{14,22},{15,23},{16,... | collective-permute-start | bytes 1966088 | tf_op jit(solution)/shard_map/ppermute | solution.py:135
  154.2 20.5 %collective-permute-start.30 = (bf16[3,128,1024]{2,1,0:T(8,128)(2,1)}, bf16[3,128,1024]{2,1,0:T(8,128)(2,1)S(1)}, u32[]{:S(2)}, u32[]{:S(2)}) collective-permute-start(bf16[3,128,1024]{2,1,0:T(8,128)(2,1)} %collective-permute-done.29), channel_id=1, source_target_pairs={{0,1},{1,0},{2,3},{3,2},{4,5},{5,4},{6,7},{7,6},{8,9},{9,8},{10,11... | collective-permute-start | bytes 2359304 | tf_op jit(solution)/shard_map/ppermute | solution.py:135
  156.9 29.0 %collective-permute-start.4 = (bf16[512,640]{1,0:T(8,128)(2,1)S(1)}, bf16[512,640]{1,0:T(8,128)(2,1)S(1)}, u32[]{:S(2)}, u32[]{:S(2)}) collective-permute-start(bf16[512,640]{1,0:T(8,128)(2,1)S(1)} %collective-permute-done.1), channel_id=1, source_target_pairs={{8,0},{9,1},{10,2},{11,3},{12,4},{13,5},{14,6},{15,7},{16,24},{17,... | collective-permute-start | bytes 1966088 | tf_op jit(solution)/shard_map/ppermute | solution.py:135
  160.2 73.2 %collective-permute-start.10 = (bf16[512,640]{1,0:T(8,128)(2,1)}, bf16[512,640]{1,0:T(8,128)(2,1)S(1)}, u32[]{:S(2)}, u32[]{:S(2)}) collective-permute-start(bf16[512,640]{1,0:T(8,128)(2,1)} %collective-permute-done.7), channel_id=1, source_target_pairs={{8,0},{9,1},{10,2},{11,3},{12,4},{13,5},{14,6},{15,7},{16,24},{17,... | collective-permute-start | bytes 1966088 | tf_op jit(solution)/shard_map/ppermute | solution.py:135
  171.9 42.1 %collective-permute-start.21 = (bf16[512,640]{1,0:T(8,128)(2,1)S(1)}, bf16[512,640]{1,0:T(8,128)(2,1)S(1)}, u32[]{:S(2)}, u32[]{:S(2)}) collective-permute-start(bf16[512,640]{1,0:T(8,128)(2,1)S(1)} %collective-permute-done.18), channel_id=1, source_target_pairs={{8,0},{9,1},{10,2},{11,3},{12,4},{13,5},{14,6},{15,7},{16,24},{17,... | collective-permute-start | bytes 1966088 | tf_op jit(solution)/shard_map/ppermute | solution.py:135
  173.2 53.4 %collective-permute-start.15 = (bf16[512,640]{1,0:T(8,128)(2,1)S(1)}, bf16[512,640]{1,0:T(8,128)(2,1)S(1)}, u32[]{:S(2)}, u32[]{:S(2)}) collective-permute-start(bf16[512,640]{1,0:T(8,128)(2,1)S(1)} %collective-permute-done.12), channel_id=1, source_target_pairs={{8,0},{9,1},{10,2},{11,3},{12,4},{13,5},{14,6},{15,7},{16,24},{17,... | collective-permute-start | bytes 1966088 | tf_op jit(solution)/shard_map/ppermute | solution.py:135
  191.3 100.6 %collective-permute-start.31 = (bf16[512,640]{1,0:T(8,128)(2,1)}, bf16[512,640]{1,0:T(8,128)(2,1)}, u32[]{:S(2)}, u32[]{:S(2)}) collective-permute-start(bf16[512,640]{1,0:T(8,128)(2,1)} %fusion.14), channel_id=1, source_target_pairs={{0,4},{1,5},{2,6},{3,7},{4,0},{5,1},{6,2},{7,3},{8,12},{9,13},{10,... | collective-permute-start | bytes 1966088 | tf_op jit(solution)/shard_map/ppermute | solution.py:135
  218.5 60.2 %collective-permute-start.44 = (bf16[512,640]{1,0:T(8,128)(2,1)}, bf16[512,640]{1,0:T(8,128)(2,1)}, u32[]{:S(2)}, u32[]{:S(2)}) collective-permute-start(bf16[512,640]{1,0:T(8,128)(2,1)} %fusion.23), channel_id=1, source_target_pairs={{0,4},{1,5},{2,6},{3,7},{4,0},{5,1},{6,2},{7,3},{8,12},{9,13},{10,... | collective-permute-start | bytes 1966088 | tf_op jit(solution)/shard_map/ppermute | solution.py:135
  232.0 54.7 %collective-permute-start.43 = (bf16[512,640]{1,0:T(8,128)(2,1)}, bf16[512,640]{1,0:T(8,128)(2,1)}, u32[]{:S(2)}, u32[]{:S(2)}) collective-permute-start(bf16[512,640]{1,0:T(8,128)(2,1)} %fusion.20), channel_id=1, source_target_pairs={{0,4},{1,5},{2,6},{3,7},{4,0},{5,1},{6,2},{7,3},{8,12},{9,13},{10,... | collective-permute-start | bytes 1966088 | tf_op jit(solution)/shard_map/ppermute | solution.py:135
  238.8 56.6 %collective-permute-start.32 = (bf16[512,640]{1,0:T(8,128)(2,1)}, bf16[512,640]{1,0:T(8,128)(2,1)}, u32[]{:S(2)}, u32[]{:S(2)}) collective-permute-start(bf16[512,640]{1,0:T(8,128)(2,1)} %fusion.17), channel_id=1, source_target_pairs={{0,4},{1,5},{2,6},{3,7},{4,0},{5,1},{6,2},{7,3},{8,12},{9,13},{10,... | collective-permute-start | bytes 1966088 | tf_op jit(solution)/shard_map/ppermute | solution.py:135
  278.6 38.6 %collective-permute-start.22 = (bf16[2,512,1024]{2,1,0:T(8,128)(2,1)}, bf16[2,512,1024]{2,1,0:T(8,128)(2,1)}, u32[]{:S(2)}, u32[]{:S(2)}) collective-permute-start(bf16[2,512,1024]{2,1,0:T(8,128)(2,1)} %fusion), channel_id=1, source_target_pairs={{0,1},{1,0},{2,3},{3,2},{4,5},{5,4},{6,7},{7,6},{8,9},{9,8},{10,11... | collective-permute-start | bytes 6291464 | tf_op jit(solution)/shard_map/ppermute | solution.py:135
  323.1 36.9 %collective-permute-start.23 = (bf16[512,1024]{1,0:T(8,128)(2,1)S(1)}, bf16[512,1024]{1,0:T(8,128)(2,1)S(1)}, u32[]{:S(2)}, u32[]{:S(2)}) collective-permute-start(bf16[512,1024]{1,0:T(8,128)(2,1)S(1)} %fusion.48), channel_id=1, source_target_pairs={{0,2},{1,3},{2,0},{3,1},{4,6},{5,7},{6,4},{7,5},{8,10},{9,11},{10,... | collective-permute-start | bytes 3145736 | tf_op jit(solution)/shard_map/ppermute | solution.py:135
  323.6 24.6 %collective-permute-start.39 = (f32[128]{0:T(128)S(1)}, f32[128]{0:T(128)S(1)}, u32[]{:S(2)}, u32[]{:S(2)}) collective-permute-start(f32[128]{0:T(128)S(1)} %broadcast_add_fusion.1), channel_id=1, source_target_pairs={{0,2},{1,3},{2,0},{3,1},{4,6},{5,7},{6,4},{7,5},{8,10},{9,11},{10,... | collective-permute-start | bytes 1544 | tf_op jit(solution)/shard_map/ppermute | solution.py:135
  325.2 24.4 %collective-permute-start.51 = (f32[128]{0:T(128)S(1)}, f32[128]{0:T(128)S(1)}, u32[]{:S(2)}, u32[]{:S(2)}) collective-permute-start(f32[128]{0:T(128)S(1)} %broadcast_add_fusion), channel_id=1, source_target_pairs={{0,2},{1,3},{2,0},{3,1},{4,6},{5,7},{6,4},{7,5},{8,10},{9,11},{10,... | collective-permute-start | bytes 1544 | tf_op jit(solution)/shard_map/ppermute | solution.py:135
  360.6 47.4 %collective-permute-start.24 = (bf16[512,1024]{1,0:T(8,128)(2,1)S(1)}, bf16[512,1024]{1,0:T(8,128)(2,1)S(1)}, u32[]{:S(2)}, u32[]{:S(2)}) collective-permute-start(bf16[512,1024]{1,0:T(8,128)(2,1)S(1)} %fusion.1), channel_id=1, source_target_pairs={{0,0},{1,8},{2,16},{3,24},{4,4},{5,12},{6,20},{7,28},{8,9},{9,1},{... | collective-permute-start | bytes 3145736 | tf_op jit(solution)/shard_map/ppermute | solution.py:135
  (59 other events, 1159.9 us)
